TPU v7x, 32 devices: a whole 2x2x4 slice. The times are simulated.
32 devices in a mesh: rows: 4 (over x, core), cols: 8 (over z, y).
Axes of the slice: x: 2, y: 2, z: 4, core: 2. Of those that a mesh axis runs over, the one named last changes fastest.
Arguments:
- object_field: float32 [2, 1024, 2048], P(None, 'rows', 'cols'), may hold values from -4 to 4
- probe_modes: float32 [4, 2, 128, 128], replicated, may hold values from -2 to 2
- intensity: float32 [512, 128, 128], P(('rows', 'cols')), may hold values from 0.25 to 1.75
- positions: int32 [512, 2], P(('rows', 'cols')), may hold values from 0 to 256
- frame_count: int32 [32], P(('rows', 'cols')), may hold values from 1 to 16, as said below
Outputs:
- object_out: float32 [2, 1024, 2048], P(None, 'rows', 'cols')
- probe_out: float32 [4, 2, 128, 128], replicated
Inputs may be any that keep to these rules, and one draw needn't show every extreme that they name: `frame_count`: some device has all 16 slots live.
All inputs are finite; a program needn't handle non-finite values.
Results may differ from a plain program's by a relative error of at most 0.0003.
Values sent between devices are 32-bit elements; how exact they have to be, the bound alone decides.
A program may use at most 128 MiB of HBM per device.

v0:
```python
from functools import partial
import math

import jax
import jax.numpy as jnp
from jax import lax
from jax.sharding import PartitionSpec as P

ITERS = 2


object_rate = 0.1
probe_rate = 2.0
highest = lax.Precision.HIGHEST


def extended_2(cells, sides, width):
    for axis, dim in sides:
        count = lax.axis_size(axis)
        ends = count - 1
        head = lax.slice_in_dim(cells, 0, width, axis=dim)
        tail = lax.slice_in_dim(cells, cells.shape[dim] - width, cells.shape[dim], axis=dim)
        cells = jnp.concatenate(
            [
                lax.ppermute(tail, axis, [(i, (i + 1) % count) for i in range(ends)]),
                cells,
                lax.ppermute(head, axis, [((i + 1) % count, i) for i in range(ends)]),
            ],
            axis=dim,
        )
    return cells


def propagator(width):
    index = jnp.arange(width, dtype=jnp.int32)
    product = index[:, None] * index[None, :] % width
    angle = 2.0 * math.pi / width * product.astype(jnp.float32)
    e_real = jnp.cos(angle)
    e_imag = jnp.sin(angle)
    freq = jnp.where(index < width // 2, index, index - width).astype(jnp.float32)
    theta = math.pi * freq * freq / width
    h_real = jnp.cos(theta)
    h_imag = -jnp.sin(theta)
    m_real = h_real[:, None] * e_real + h_imag[:, None] * e_imag
    m_imag = h_imag[:, None] * e_real - h_real[:, None] * e_imag
    matmul = partial(jnp.dot, precision=highest)
    k_real = (matmul(e_real, m_real) - matmul(e_imag, m_imag)) / width
    k_imag = (matmul(e_real, m_imag) + matmul(e_imag, m_real)) / width
    return (k_real, k_imag)


def left_mult(matrix, field):
    return jnp.einsum("ij,smjk->smik", matrix, field, precision=highest)


def right_mult(field, matrix):
    return jnp.einsum("smij,jk->smik", field, matrix, precision=highest)


def block_pass(extended, probe, k_real, k_imag, positions, intensity, count, first, size):
    width = probe.shape[-1]
    p_real = probe[:, 0][None]
    p_imag = probe[:, 1][None]

    def take(row0, col0):
        return lax.dynamic_slice(extended, (jnp.int32(0), row0, col0), (2, width, width))

    patches = jax.vmap(take)(positions[:, 0], positions[:, 1])
    o_real = patches[:, 0][:, None]
    o_imag = patches[:, 1][:, None]
    x_real = p_real * o_real - p_imag * o_imag
    x_imag = p_real * o_imag + p_imag * o_real
    a_real = left_mult(k_real, x_real) - left_mult(k_imag, x_imag)
    a_imag = left_mult(k_real, x_imag) + left_mult(k_imag, x_real)
    w_real = right_mult(a_real, k_real) - right_mult(a_imag, k_imag)
    w_imag = right_mult(a_real, k_imag) + right_mult(a_imag, k_real)
    inten = jnp.sum(w_real * w_real + w_imag * w_imag, axis=1)
    slot_ids = first + jnp.arange(size, dtype=jnp.int32)
    live = (slot_ids < count).astype(jnp.float32)
    resid = 4.0 * (inten - intensity) * live[:, None, None]
    g_real = resid[:, None] * w_real
    g_imag = resid[:, None] * w_imag
    c_real = left_mult(k_real, g_real) + left_mult(k_imag, g_imag)
    c_imag = left_mult(k_real, g_imag) - left_mult(k_imag, g_real)
    d_real = right_mult(c_real, k_real) + right_mult(c_imag, k_imag)
    d_imag = right_mult(c_imag, k_real) - right_mult(c_real, k_imag)
    go_real = jnp.sum(p_real * d_real + p_imag * d_imag, axis=1)
    go_imag = jnp.sum(p_real * d_imag - p_imag * d_real, axis=1)
    gp_real = jnp.sum(o_real * d_real + o_imag * d_imag, axis=0)
    gp_imag = jnp.sum(o_real * d_imag - o_imag * d_real, axis=0)
    gradients = jnp.stack([go_real, go_imag], axis=1)
    return (gradients, positions, jnp.stack([gp_real, gp_imag], axis=1))


def frame_pass(extended, probe, k_real, k_imag, positions, intensity, count, blocks, size):
    width = probe.shape[-1]

    def block_step(block, carry):
        gext, gprobe = carry
        first = (block * size).astype(jnp.int32)
        gradients, where, gpart = block_pass(
            extended, probe, k_real, k_imag, positions, intensity, count, first, size
        )

        def add_one(item, acc):
            row0 = where[item, 0]
            col0 = where[item, 1]
            current = lax.dynamic_slice(acc, (jnp.int32(0), row0, col0), (2, width, width))
            return lax.dynamic_update_slice(
                acc, current + gradients[item], (jnp.int32(0), row0, col0)
            )

        gext = lax.fori_loop(0, size, add_one, gext)
        return (gext, gprobe + gpart)

    init = (jnp.zeros(extended.shape, jnp.float32), jnp.zeros(probe.shape, jnp.float32))
    return lax.fori_loop(0, blocks, block_step, init)


def fold_rims(padded, dim, start, length, width):
    total = padded.shape[dim]
    core = lax.slice_in_dim(padded, start, start + length, axis=dim)
    low = lax.slice_in_dim(padded, 0, width, axis=dim)
    high = lax.slice_in_dim(padded, total - width, total, axis=dim)
    low_pad = [(0, 0)] * padded.ndim
    high_pad = [(0, 0)] * padded.ndim
    low_pad[dim] = (0, length - width)
    high_pad[dim] = (length - width, 0)
    return core + jnp.pad(low, low_pad) + jnp.pad(high, high_pad)


def fetch_object(tile_field, half):
    return extended_2(tile_field, (("rows", 1), ("cols", 2)), half)


def return_gradient(gext, tile, width, half):
    padded = extended_2(gext, (("rows", 1), ("cols", 2)), half)
    folded = fold_rims(padded, 1, width, tile, half)
    return fold_rims(folded, 2, width, tile, half)


def body(object_field, probe_modes, intensity, positions, frame_count):
    tile = object_field.shape[1]
    width = probe_modes.shape[-1]
    half = width // 2
    slots = positions.shape[0]
    row_count = lax.axis_size("rows")
    col_count = lax.axis_size("cols")
    frames_all = slots * row_count * col_count
    k_real, k_imag = propagator(width)
    count = frame_count[0]
    blocks = 1
    probe = probe_modes
    tile_field = object_field
    extended = fetch_object(tile_field, half)
    for it in range(ITERS):
        last = it == ITERS - 1
        gext, gprobe = frame_pass(
            extended, probe, k_real, k_imag, positions, intensity, count, blocks, slots
        )
        total = lax.psum(gprobe, ("rows", "cols"))
        probe = probe - probe_rate / frames_all * total
        if not last:
            padded = extended_2(gext, (("rows", 1), ("cols", 2)), width)
            folded = fold_rims(padded, 1, width, tile + width, width)
            full = fold_rims(folded, 2, width, tile + width, width)
            offsets = jnp.arange(tile + width, dtype=jnp.int32) - half
            row_pixel = lax.axis_index("rows") * tile + offsets
            col_pixel = lax.axis_index("cols") * tile + offsets
            row_inside = ((row_pixel >= 0) & (row_pixel < tile * row_count)).astype(jnp.float32)
            col_inside = ((col_pixel >= 0) & (col_pixel < tile * col_count)).astype(jnp.float32)
            inside = row_inside[:, None] * col_inside[None, :]
            extended = extended - object_rate * full * inside[None]
            tile_field = extended[:, half : half + tile, half : half + tile]
        else:
            gradient = return_gradient(gext, tile, width, half)
            tile_field = tile_field - object_rate * gradient
    return (tile_field, probe)


def solution(mesh):
    return jax.shard_map(
        body,
        mesh=mesh,
        in_specs=(
            P(None, "rows", "cols"),
            P(),
            P(("rows", "cols"), None, None),
            P(("rows", "cols"), None),
            P(("rows", "cols")),
        ),
        out_specs=(P(None, "rows", "cols"), P()),
        check_vma=False,
    )
```

profile of v0, /device:TPU:0, one launch (start us, length us, event | category | flops | bytes accessed | tf_op | source)
XLA Modules:
  0.0 881.4 jit_solution(7850431220355603628)
XLA Ops:
  22.4 15.1 %collective-permute-done.2 = f32[2,384,64]{2,1,0:T(8,128)S(1)} collective-permute-done((f32[2,384,64]{2,1,0:T(8,128)S(1)}, f32[2,384,64]{2,1,0:T(8,128)S(1)}, u32[]{:S(2)}, u32[]{:S(2)}) %collective-permute-start.2) | collective-permute-done | bytes 196640 | tf_op jit(solution)/shard_map/ppermute | solution.py:25
  39.2 46.1 %while.48 = (s32[]{:T(128)}, f32[2,384,384]{2,1,0:T(8,128)}, s32[16,3]{0,1:T(4,128)S(1)}, f32[16,2,128,128]{3,2,1,0:T(8,128)S(1)}, s32[]{:T(128)}) while((s32[]{:T(128)}, f32[2,384,384]{2,1,0:T(8,128)}, s32[16,3]{0,1:T(4,128)S(1)}, f32[16,2,128,128]{3,2,1,0:T(8,128)S(1)}, s32[]{:T(128)}) %tuple.118), condition=%wide.while_cond, body=%wide.while_body.sunk | while | flops 2 | bytes 262261 | solution.py:66
  92.4 7.2 fusion.37
  99.6 7.1 fusion.123
  106.7 7.1 fusion.26
  120.5 7.2 fusion.122
  127.8 7.2 fusion.56
  142.3 7.3 fusion.50
  170.2 7.1 fusion.16
  177.3 7.1 fusion.80
  191.1 10.8 %add_reduce_fusion.3 = (f32[4,128,128]{2,1,0:T(8,128)}, f32[4,128,128]{2,1,0:T(8,128)}, f32[16,128,128]{2,1,0:T(8,128)S(1)}, f32[16,128,128]{2,1,0:T(8,128)S(1)}) fusion(f32[16,4,128,128]{3,2,1,0:T(8,128)S(1)} %fusion.62, f32[16,128,128]{2,1,0:T(8,128)S(1)} %get-tuple-element.311, f32[16,128,128]{2,1,0:T(8,128)S(1)} %get-tuple-element.310, ...), kind=kOutput, calls=%fused_computation.54 | convolution fusion | flops 1627783168 | bytes 17891328 | tf_op jit(solution)/shard_map/while/body/eval_jaxpr/smij,jk->smik/dot_general | solution.py:57
  202.6 115.6 %while.46 = (s32[]{:T(128)}, f32[2,384,384]{2,1,0:T(8,128)S(1)}, s32[16,2]{0,1:T(2,128)S(1)}, f32[16,2,128,128]{3,2,1,0:T(8,128)S(1)}, s32[]{:T(128)}, /*index=5*/s32[]{:T(128)}, s32[]{:T(128)}) while((s32[]{:T(128)}, f32[2,384,384]{2,1,0:T(8,128)S(1)}, s32[16,2]{0,1:T(2,128)S(1)}, f32[16,2,128,128]{3,2,1,0:T(8,128)S(1)}, s32[]{:T(128)}, ...), condition=%wide.region_4.5_spmd, body=%wide.region_3.4_spmd.sunk | while | flops 32776 | bytes 655541 | solution.py:113
  338.4 121.8 %all-reduce.7.cloned.1.call-done = f32[4,2,128,128]{3,2,1,0:T(8,128)} async-done(((f32[4,2,128,128]{3,2,1,0:T(8,128)}), f32[4,2,128,128]{3,2,1,0:T(8,128)}) %all-reduce.7.cloned.1.call-update) | async-done | bytes 524304 | tf_op jit(solution)/shard_map/psum | solution.py:161
  466.8 46.6 %while.49 = (s32[]{:T(128)}, f32[2,384,384]{2,1,0:T(8,128)}, s32[16,3]{0,1:T(4,128)S(1)}, f32[16,2,128,128]{3,2,1,0:T(8,128)S(1)}, s32[]{:T(128)}) while((s32[]{:T(128)}, f32[2,384,384]{2,1,0:T(8,128)}, s32[16,3]{0,1:T(4,128)S(1)}, f32[16,2,128,128]{3,2,1,0:T(8,128)S(1)}, s32[]{:T(128)}) %tuple.134), condition=%wide.while_cond.1, body=%wide.while_body.1.sunk | while | flops 2 | bytes 262261 | solution.py:66
  520.5 7.2 fusion.32
  527.7 7.1 fusion.101
  548.3 7.5 fusion.100
  555.8 7.1 fusion.68
  570.3 7.1 fusion.42
  584.3 7.3 fusion.89
  605.1 7.1 fusion.86
  619.0 10.8 %add_reduce_fusion = (f32[4,128,128]{2,1,0:T(8,128)}, f32[4,128,128]{2,1,0:T(8,128)}, f32[16,128,128]{2,1,0:T(8,128)S(1)}, f32[16,128,128]{2,1,0:T(8,128)S(1)}) fusion(f32[16,4,128,128]{3,2,1,0:T(8,128)S(1)} %fusion.74, f32[16,128,128]{2,1,0:T(8,128)S(1)} %get-tuple-element.309, f32[16,128,128]{2,1,0:T(8,128)S(1)} %get-tuple-element.308, ...), kind=kOutput, calls=%fused_computation.43 | convolution fusion | flops 1627783168 | bytes 17891328 | tf_op jit(solution)/shard_map/while/body/eval_jaxpr/smij,jk->smik/dot_general | solution.py:57
  630.0 106.5 %while.47 = (s32[]{:T(128)}, f32[2,384,384]{2,1,0:T(8,128)S(1)}, s32[16,2]{0,1:T(2,128)S(1)}, f32[16,2,128,128]{3,2,1,0:T(8,128)S(1)}, s32[]{:T(128)}, /*index=5*/s32[]{:T(128)}, s32[]{:T(128)}) while((s32[]{:T(128)}, f32[2,384,384]{2,1,0:T(8,128)S(1)}, s32[16,2]{0,1:T(2,128)S(1)}, f32[16,2,128,128]{3,2,1,0:T(8,128)S(1)}, s32[]{:T(128)}, ...), condition=%wide.region_12.13_spmd, body=%wide.region_11.12_spmd.sunk | while | flops 32776 | bytes 655541 | solution.py:113
  752.4 116.5 %all-reduce.9.cloned.1.call-done = f32[4,2,128,128]{3,2,1,0:T(8,128)} async-done(((f32[4,2,128,128]{3,2,1,0:T(8,128)}), f32[4,2,128,128]{3,2,1,0:T(8,128)}) %all-reduce.9.cloned.1.call-update) | async-done | bytes 524304 | tf_op jit(solution)/shard_map/psum | solution.py:161
  (315 shorter events, 360.7 us)
Async XLA Ops:
  7.2 15.1 %copy-start.7 = (f32[4,2,128,128]{3,2,1,0:T(8,128)S(1)}, f32[4,2,128,128]{3,2,1,0:T(8,128)}, u32[]{:S(2)}) copy-start(f32[4,2,128,128]{3,2,1,0:T(8,128)} %param.10) | copy-start | bytes 1572868
  7.2 453.1 %all-reduce.7.cloned.1.call-start = ((), (), s32[]{:S(2)}) async-start(), calls=%async_computation | async-start | bytes 1048576 | tf_op jit(solution)/shard_map/psum | solution.py:161
  8.3 7.1 collective-permute-start
  10.6 5.9 collective-permute-start.1
  16.5 20.9 %copy-start = (f32[2,384,256]{2,1,0:T(8,128)}, f32[2,384,256]{2,1,0:T(8,128)S(1)}, u32[]{:S(2)}) copy-start(f32[2,384,256]{2,1,0:T(8,128)S(1)} %constant_dynamic-update-slice_fusion) | copy-start | bytes 2359300
  16.7 20.7 %collective-permute-start.2 = (f32[2,384,64]{2,1,0:T(8,128)S(1)}, f32[2,384,64]{2,1,0:T(8,128)S(1)}, u32[]{:S(2)}, u32[]{:S(2)}) collective-permute-start(f32[2,384,64]{2,1,0:T(8,128)S(1)} %get-tuple-element.320), channel_id=1, source_target_pairs={{0,1},{1,2},{2,3},{3,4},{4,5},{5,6},{6,7},{8,9},{9,10},{10,11},{11... | collective-permute-start | bytes 589832 | tf_op jit(solution)/shard_map/ppermute | solution.py:25
  21.0 16.4 %collective-permute-start.3 = (f32[2,384,64]{2,1,0:T(8,128)S(1)}, f32[2,384,64]{2,1,0:T(8,128)S(1)}, u32[]{:S(2)}, u32[]{:S(2)}) collective-permute-start(f32[2,384,64]{2,1,0:T(8,128)S(1)} %get-tuple-element.321), channel_id=1, source_target_pairs={{1,0},{2,1},{3,2},{4,3},{5,4},{6,5},{7,6},{9,8},{10,9},{11,10},{12... | collective-permute-start | bytes 589832 | tf_op jit(solution)/shard_map/ppermute | solution.py:27
  37.4 1.8 copy-start.10
  134.9 7.1 copy-start.4
  319.0 7.6 collective-permute-start.4
  323.4 5.3 collective-permute-start.5
  326.5 542.4 %all-reduce.9.cloned.1.call-start = ((), (), s32[]{:S(2)}) async-start(), calls=%async_computation.1 | async-start | bytes 1048576 | tf_op jit(solution)/shard_map/psum | solution.py:161
  330.8 130.7 %collective-permute-start.6 = (f32[2,640,128]{2,1,0:T(8,128)}, f32[2,640,128]{2,1,0:T(8,128)}, u32[]{:S(2)}, u32[]{:S(2)}) collective-permute-start(f32[2,640,128]{2,1,0:T(8,128)} %get-tuple-element.312), channel_id=1, source_target_pairs={{0,1},{1,2},{2,3},{3,4},{4,5},{5,6},{6,7},{8,9},{9,10},{10,11},{11... | collective-permute-start | bytes 1966088 | tf_op jit(solution)/shard_map/ppermute | solution.py:25
  336.2 125.4 %collective-permute-start.7 = (f32[2,640,128]{2,1,0:T(8,128)}, f32[2,640,128]{2,1,0:T(8,128)}, u32[]{:S(2)}, u32[]{:S(2)}) collective-permute-start(f32[2,640,128]{2,1,0:T(8,128)} %get-tuple-element.313), channel_id=1, source_target_pairs={{1,0},{2,1},{3,2},{4,3},{5,4},{6,5},{7,6},{9,8},{10,9},{11,10},{12... | collective-permute-start | bytes 1966088 | tf_op jit(solution)/shard_map/ppermute | solution.py:27
  338.4 124.8 %copy-start.14 = (pred[384]{0:T(512)(128)(4,1)S(1)}, pred[384]{0:T(512)(128)(4,1)}, u32[]{:S(2)}) copy-start(pred[384]{0:T(512)(128)(4,1)} %constant.143.clone.1) | copy-start | bytes 1156
  461.5 3.3 copy-start.2
  463.3 1.7 copy-start.11
  563.0 7.1 copy-start.5
  736.4 132.5 %copy-start.3 = (f32[4,2,128,128]{3,2,1,0:T(8,128)S(1)}, f32[4,2,128,128]{3,2,1,0:T(8,128)}, u32[]{:S(2)}) copy-start(f32[4,2,128,128]{3,2,1,0:T(8,128)} %copy-done.2) | copy-start | bytes 1572868
  737.2 5.2 collective-permute-start.8
  741.0 5.5 collective-permute-start.9
  746.5 125.1 %copy-start.13 = (pred[256]{0:T(512)(128)(4,1)S(1)}, pred[256]{0:T(512)(128)(4,1)}, u32[]{:S(2)}) copy-start(pred[256]{0:T(512)(128)(4,1)} %constant.152.clone.1) | copy-start | bytes 772
  747.6 123.2 %collective-permute-start.10 = (f32[2,512,64]{2,1,0:T(8,128)}, f32[2,512,64]{2,1,0:T(8,128)S(1)}, u32[]{:S(2)}, u32[]{:S(2)}) collective-permute-start(f32[2,512,64]{2,1,0:T(8,128)} %get-tuple-element.314), channel_id=1, source_target_pairs={{0,1},{1,2},{2,3},{3,4},{4,5},{5,6},{6,7},{8,9},{9,10},{10,11},{11... | collective-permute-start | bytes 786440 | tf_op jit(solution)/shard_map/ppermute | solution.py:25
  751.1 119.7 %collective-permute-start.11 = (f32[2,512,64]{2,1,0:T(8,128)}, f32[2,512,64]{2,1,0:T(8,128)S(1)}, u32[]{:S(2)}, u32[]{:S(2)}) collective-permute-start(f32[2,512,64]{2,1,0:T(8,128)} %get-tuple-element.315), channel_id=1, source_target_pairs={{1,0},{2,1},{3,2},{4,3},{5,4},{6,5},{7,6},{9,8},{10,9},{11,10},{12... | collective-permute-start | bytes 786440 | tf_op jit(solution)/shard_map/ppermute | solution.py:27
  (5 other events, 7.1 us)
Sparse Core Ops, SparseCore 0:
  326.7 133.5 all-reduce.6
  741.2 127.7 all-reduce.8
where the time goes:
time: 889 us; the launch traced here: 881 us
  waiting for transfers between devices  257 us (29%)
  matrix products  234 us (26%)
  local copies, waits for them, and re-layouts  200 us (22%)
  loops' own time  122 us (14%)
  starting transfers between devices  29.7 us (3%)
  other arithmetic  22.5 us (3%)
  between operations  15.8 us (2%)
    psum x2, waiting for transfers between devices, body(): total = lax.psum(gprobe, ('rows', 'cols'))  238 us
    another operation x2, loops' own time, block_step(): gext = lax.fori_loop(0, size, add_one, gext)  121 us
    dot_general x16, matrix products, right_mult(): return jnp.einsum('smij,jk->smik', field, matrix, precision=highest)  118 us
    dot_general x16, matrix products, left_mult(): return jnp.einsum('ij,smjk->smik', matrix, field, precision=highest)  114 us
    gather x96, local copies, waits for them, and re-layouts  91.5 us
    dynamic_update_slice x32, local copies, waits for them, and re-layouts, add_one(): lax.dynamic_update_slice(acc, current + gradients[item], (jnp.int32(0), r...  76.7 us
    ppermute x6, starting transfers between devices, extended_2(): lax.ppermute(tail, axis, [(i, (i + 1) % count) for i in range(ends)])  21.9 us
    dynamic_slice x32, local copies, waits for them, and re-layouts, add_one(): col0 = where[item, 1]  20.6 us
  transfers between devices with their start and end apart: 14, of which 5 were waited for; matrix products, arithmetic and copies ran while one was open for 2% of the time, Pallas kernels for 0%

commit v1 on v0

v1 whole, which is shorter than its diff:
```python
from functools import partial
import math

import jax
import jax.numpy as jnp
import numpy as np
from jax import lax
from jax.experimental import pallas as pl
from jax.experimental.pallas import tpu as pltpu
from jax.sharding import PartitionSpec as P

ITERS = 2
object_rate = 0.1
probe_rate = 2.0
f32 = jnp.float32
bf16 = jnp.bfloat16


def extended_2(cells, sides, width):
    for axis, dim in sides:
        count = lax.axis_size(axis)
        ends = count - 1
        head = lax.slice_in_dim(cells, 0, width, axis=dim)
        tail = lax.slice_in_dim(cells, cells.shape[dim] - width, cells.shape[dim], axis=dim)
        cells = jnp.concatenate(
            [
                lax.ppermute(tail, axis, [(i, (i + 1) % count) for i in range(ends)]),
                cells,
                lax.ppermute(head, axis, [((i + 1) % count, i) for i in range(ends)]),
            ],
            axis=dim,
        )
    return cells


def chirp(width):
    j = np.arange(width)
    turn = (j * j) % (2 * width)
    angle = math.pi * ((turn[:, None] + turn[None, :]) % (2 * width)) / width
    return np.cos(angle).astype(np.float32), np.sin(angle).astype(np.float32)


def split_np(matrix):
    high = matrix.astype(np.float32).astype(bf16)
    low = (matrix - high.astype(np.float64)).astype(np.float32).astype(bf16)
    return np.asarray(high), np.asarray(low)


def transforms(width):
    j = np.arange(width)
    angle = 2.0 * math.pi * ((j[:, None] * j[None, :]) % width) / width
    c, s = np.cos(angle) / math.sqrt(width), np.sin(angle) / math.sqrt(width)
    plus = np.block([[c, -s], [s, c]])
    minus = np.block([[c, s], [-s, c]])
    out = []
    for m in (plus, minus):
        high, low = split_np(m)
        out.append(np.concatenate([high, high, low], axis=0))
    for m in (minus, plus):
        high, low = split_np(m)
        out.append(np.concatenate([high, high, low], axis=1))
    return out


def split(x):
    high = x.astype(bf16)
    return high, (x - high.astype(f32)).astype(bf16)


def right(x, weights):
    high, low = split(x)
    return jnp.dot(
        jnp.concatenate([high, low, high], axis=1), weights, preferred_element_type=f32
    )


def left(weights, x):
    high, low = split(x)
    return jnp.dot(
        weights, jnp.concatenate([high, low, high], axis=0), preferred_element_type=f32
    )


def frames_kernel(
    modes, width, step, pos, count, ext, probe, inten, rf, ra, lf, la, gext, gprobe
):
    slots = inten.shape[0]
    tall = width + 8
    gext[...] = jnp.zeros_like(gext)
    gprobe[...] = jnp.zeros_like(gprobe)

    def place(frame):
        row = pos[frame, 0]
        col = pos[frame, 1]
        top = pl.multiple_of(jnp.minimum(row // 8, (ext.shape[1] - tall) // 8) * 8, 8)
        base = pl.multiple_of(jnp.minimum(col // width, 1) * width, width)
        return top, row - top, base, col - base

    def moved(x, by, axis):
        return pltpu.roll(x, jnp.where(by == 0, 0, x.shape[axis] - by), axis)

    def frame_gradient(frame):
        top, down, base, shift = place(frame)
        o_r, o_i = [
            moved(
                moved(ext[k, pl.ds(top, tall), pl.ds(base, 2 * width)], shift, 1)[:, :width],
                down,
                0,
            )[:width]
            for k in range(2)
        ]
        x = []
        for m in range(modes):
            p_r, p_i = probe[m, 0], probe[m, 1]
            x.append(jnp.concatenate([p_r * o_r - p_i * o_i, p_r * o_i + p_i * o_r], axis=1))
        z = right(jnp.concatenate(x, axis=0), rf[...])
        z = jnp.concatenate(
            [
                jnp.concatenate(
                    [z[m * width : (m + 1) * width, :width], z[m * width : (m + 1) * width, width:]],
                    axis=0,
                )
                for m in range(modes)
            ],
            axis=1,
        )
        y = left(lf[...], z)
        power = y * y
        total = power[:width] + power[width:]
        i_sum = sum(total[:, m * width : (m + 1) * width] for m in range(modes))
        live = jnp.where(frame < count[0], 4.0, 0.0).astype(f32)
        e = live * (i_sum - inten[frame])
        e = jnp.concatenate([e] * modes, axis=1)
        w = y * jnp.concatenate([e, e], axis=0)
        v = left(la[...], w)
        v = jnp.concatenate(
            [
                jnp.concatenate(
                    [v[:width, m * width : (m + 1) * width], v[width:, m * width : (m + 1) * width]],
                    axis=1,
                )
                for m in range(modes)
            ],
            axis=0,
        )
        d = right(v, ra[...])
        go_r = go_i = 0.0
        parts = []
        for m in range(modes):
            d_r = d[m * width : (m + 1) * width, :width]
            d_i = d[m * width : (m + 1) * width, width:]
            p_r, p_i = probe[m, 0], probe[m, 1]
            go_r += p_r * d_r + p_i * d_i
            go_i += p_r * d_i - p_i * d_r
            parts.append((o_r * d_r + o_i * d_i, o_r * d_i - o_i * d_r))
        return (go_r, go_i), parts

    def body(block, carry):
        frames = [block * step + k for k in range(step)]
        results = [frame_gradient(frame) for frame in frames]
        for m in range(modes):
            for k in range(2):
                gprobe[m, k] += sum(parts[m][k] for _, parts in results)
        for frame, (grad, _) in zip(frames, results):
            top, down, base, shift = place(frame)
            for k in range(2):
                wide = jnp.concatenate([grad[k], jnp.zeros((8, width), f32)], axis=0)
                wide = pltpu.roll(wide, down, 0)
                wide = jnp.concatenate([wide, jnp.zeros_like(wide)], axis=1)
                wide = pltpu.roll(wide, shift, 1)
                where = (k, pl.ds(top, tall), pl.ds(base, 2 * width))
                gext[where] += wide
        return carry

    lax.fori_loop(0, slots // step, body, 0)


def frame_pass(extended, probe, positions, intensity, count, step=4):
    modes, _, width, _ = probe.shape
    weights = [jnp.asarray(w) for w in transforms(width)]
    vmem = pl.BlockSpec(memory_space=pltpu.VMEM)
    smem = pl.BlockSpec(memory_space=pltpu.SMEM)
    slots = intensity.shape[0]
    return pl.pallas_call(
        partial(frames_kernel, modes, width, step),
        out_shape=(
            jax.ShapeDtypeStruct(extended.shape, f32),
            jax.ShapeDtypeStruct(probe.shape, f32),
        ),
        in_specs=[smem, smem] + [vmem] * 7,
        out_specs=(vmem, vmem),
        compiler_params=pltpu.CompilerParams(vmem_limit_bytes=48 * 1024 * 1024),
        cost_estimate=pl.CostEstimate(
            flops=slots * modes * 4 * 3 * 2 * width * 4 * width * width,
            bytes_accessed=4 * (extended.size * 2 + probe.size * 2 + intensity.size),
            transcendentals=0,
        ),
    )(positions, count, extended, probe, intensity, *weights)


def fold_rims(padded, dim, start, length, width):
    total = padded.shape[dim]
    core = lax.slice_in_dim(padded, start, start + length, axis=dim)
    low = lax.slice_in_dim(padded, 0, width, axis=dim)
    high = lax.slice_in_dim(padded, total - width, total, axis=dim)
    low_pad = [(0, 0)] * padded.ndim
    high_pad = [(0, 0)] * padded.ndim
    low_pad[dim] = (0, length - width)
    high_pad[dim] = (length - width, 0)
    return core + jnp.pad(low, low_pad) + jnp.pad(high, high_pad)


SIDES = (("rows", 1), ("cols", 2))


def return_gradient(gext, tile, width, half):
    padded = extended_2(gext, SIDES, half)
    folded = fold_rims(padded, 1, width, tile, half)
    return fold_rims(folded, 2, width, tile, half)


def times(field, c_real, c_imag):
    real, imag = field[:, 0], field[:, 1]
    return jnp.stack([real * c_real - imag * c_imag, real * c_imag + imag * c_real], axis=1)


def body(object_field, probe_modes, intensity, positions, frame_count):
    tile = object_field.shape[1]
    width = probe_modes.shape[-1]
    half = width // 2
    slots = positions.shape[0]
    row_count = lax.axis_size("rows")
    col_count = lax.axis_size("cols")
    frames_all = slots * row_count * col_count
    c_real, c_imag = chirp(width)
    probe = times(probe_modes, c_real, c_imag)
    tile_field = object_field
    extended = extended_2(tile_field, SIDES, half)
    for it in range(ITERS):
        last = it == ITERS - 1
        gext, gprobe = frame_pass(extended, probe, positions, intensity, frame_count)
        total = lax.psum(gprobe, ("rows", "cols"))
        probe = probe - probe_rate / frames_all * total
        gradient = return_gradient(gext, tile, width, half)
        tile_field = tile_field - object_rate * gradient
        if not last:
            extended = extended_2(tile_field, SIDES, half)
    return (tile_field, times(probe, c_real, -c_imag))


def solution(mesh):
    return jax.shard_map(
        body,
        mesh=mesh,
        in_specs=(
            P(None, "rows", "cols"),
            P(),
            P(("rows", "cols"), None, None),
            P(("rows", "cols"), None),
            P(("rows", "cols")),
        ),
        out_specs=(P(None, "rows", "cols"), P()),
        check_vma=False,
    )
```

time: 889 us -> 407 us (0.46)
  matrix products: 234 us -> 0 us
  local copies, waits for them, and re-layouts: 200 us -> 8.3 us
  loops' own time: 122 us -> 0 us
  Pallas kernels: 0 us -> 48.7 us
  waiting for transfers between devices: 257 us -> 283 us
  other arithmetic: 22.5 us -> 9.73 us
  starting transfers between devices: 29.7 us -> 40.5 us
    dot_general x36 -> x0, matrix products: 234 us -> none  [the longest x16 118 us: right_mult(): return jnp.einsum('smij,jk->smik', field, matrix, precision=highest)]
    another operation x4 -> x0, loops' own time: 122 us -> none  [the longest x2 121 us: block_step(): gext = lax.fori_loop(0, size, add_one, gext)]
    gather x96 -> x0, local copies, waits for them, and re-layouts: 91.5 us -> none
    dynamic_update_slice x32 -> x0, local copies, waits for them, and re-layouts: 76.7 us -> none  [add_one(): lax.dynamic_update_slice(acc, current + gradients[item], (jnp.int32(0), r...]
    pallas_call x0 -> x2, Pallas kernels: none -> 48.7 us  [frame_pass(): pl.pallas_call(partial(frames_kernel, modes, width, step), out_shape=(jax...]
    dynamic_slice x32 -> x0, local copies, waits for them, and re-layouts: 20.6 us -> none  [add_one(): col0 = where[item, 1]]
    ppermute x6 -> x8, waiting for transfers between devices: 15.1 us -> 31.8 us  [extended_2(): lax.ppermute(tail, axis, [(i, (i + 1) % count) for i in range(ends)])]
    ppermute x6 -> x8, starting transfers between devices: 21.9 us -> 29.8 us  [extended_2(): lax.ppermute(tail, axis, [(i, (i + 1) % count) for i in range(ends)])]
  transfers between devices with their start and end apart: 14 -> 18, of which waited for: 5 -> 8; matrix products, arithmetic and copies ran while one was open for 2% -> 2% of each run, Pallas kernels for 0% -> 0%
where the time goes in v1:
time: 407 us; the launch traced here: 406 us
  waiting for transfers between devices  283 us (70%)
  Pallas kernels  48.7 us (12%)
  starting transfers between devices  40.5 us (10%)
  between operations  15.4 us (4%)
  other arithmetic  9.73 us (2%)
  local copies, waits for them, and re-layouts  8.3 us (2%)
    psum x2, waiting for transfers between devices, body(): total = lax.psum(gprobe, ('rows', 'cols'))  241 us
    pallas_call x2, Pallas kernels, frame_pass(): pl.pallas_call(partial(frames_kernel, modes, width, step), out_shape=(jax...  48.7 us
    ppermute x8, waiting for transfers between devices, extended_2(): lax.ppermute(tail, axis, [(i, (i + 1) % count) for i in range(ends)])  31.8 us
    ppermute x8, starting transfers between devices, extended_2(): lax.ppermute(tail, axis, [(i, (i + 1) % count) for i in range(ends)])  29.8 us
    ppermute x8, starting transfers between devices, extended_2(): lax.ppermute(head, axis, [((i + 1) % count, i) for i in range(ends)])  10.6 us
    ppermute x8, waiting for transfers between devices, extended_2(): lax.ppermute(head, axis, [((i + 1) % count, i) for i in range(ends)])  10.5 us
  transfers between devices with their start and end apart: 18, of which 8 were waited for; matrix products, arithmetic and copies ran while one was open for 2% of the time, Pallas kernels for 0%

profile of v1, /device:TPU:0, one launch (start us, length us, event | category | flops | bytes accessed | tf_op | source)
XLA Modules:
  0.0 406.0 jit_solution(18259882374617183687)
XLA Ops:
  8.2 2.4 collective-permute-start
  10.6 1.4 collective-permute-start.1
  13.2 2.9 collective-permute-done.1
  17.1 4.2 %collective-permute-start.2 = (f32[2,384,64]{2,1,0:T(8,128)}, f32[2,384,64]{2,1,0:T(8,128)}, u32[]{:S(2)}, u32[]{:S(2)}) collective-permute-start(f32[2,384,64]{2,1,0:T(8,128)} %get-tuple-element.20), channel_id=1, source_target_pairs={{0,1},{1,2},{2,3},{3,4},{4,5},{5,6},{6,7},{8,9},{9,10},{10,11},{11... | collective-permute-start | bytes 589832 | tf_op jit(solution)/shard_map/ppermute | solution.py:27
  23.7 12.4 %collective-permute-done.2 = f32[2,384,64]{2,1,0:T(8,128)} collective-permute-done((f32[2,384,64]{2,1,0:T(8,128)}, f32[2,384,64]{2,1,0:T(8,128)}, u32[]{:S(2)}, u32[]{:S(2)}) %collective-permute-start.2) | collective-permute-done | bytes 196640 | tf_op jit(solution)/shard_map/ppermute | solution.py:27
  36.1 1.6 pad_maximum_fusion.2.ext
  37.8 24.3 %shard_map.167 = (f32[2,384,384]{2,1,0:T(8,128)S(1)}, f32[4,2,128,128]{3,2,1,0:T(8,128)}) custom-call(s32[16,2]{1,0:T(8,128)S(1)} %copy.18.pos, s32[1]{0:T(128)S(6)} %copy.28.count, f32[2,384,384]{2,1,0:T(8,128)S(1)} %pad_maximum_fusion.2.ext, f32[4,2,128,128]{3,2,1,0:T(8,128)S(1)} %pad_maximum_fusion.5.probe, f32[16,128,128]{2,1,0:T(8,128)S(1)} %copy-done, ...), custom_call_target="tpu_custom_call" | custom-call | flops 12884901888 | bytes 4456448 | tf_op jit(solution)/shard_map/pallas_call | solution.py:184
  62.1 4.7 %collective-permute-start.4 = (f32[2,64,384]{2,1,0:T(8,128)S(1)}, f32[2,64,384]{2,1,0:T(8,128)S(1)}, u32[]{:S(2)}, u32[]{:S(2)}) collective-permute-start(f32[2,64,384]{2,1,0:T(8,128)S(1)} %get-tuple-element.17), channel_id=1, source_target_pairs={{0,8},{8,16},{16,24},{1,9},{9,17},{17,25},{2,10},{10,18},{18,26},{... | collective-permute-start | bytes 589832 | tf_op jit(solution)/shard_map/ppermute | solution.py:27
  66.8 1.3 collective-permute-start.5
  68.2 1.9 collective-permute-done.5
  70.4 4.1 %collective-permute-start.6 = (f32[2,512,64]{2,1,0:T(8,128)S(1)}, f32[2,512,64]{2,1,0:T(8,128)S(1)}, u32[]{:S(2)}, u32[]{:S(2)}) collective-permute-start(f32[2,512,64]{2,1,0:T(8,128)S(1)} %get-tuple-element.12), channel_id=1, source_target_pairs={{0,1},{1,2},{2,3},{3,4},{4,5},{5,6},{6,7},{8,9},{9,10},{10,11},{11... | collective-permute-start | bytes 786440 | tf_op jit(solution)/shard_map/ppermute | solution.py:27
  75.8 19.4 %collective-permute-done.6 = f32[2,512,64]{2,1,0:T(8,128)S(1)} collective-permute-done((f32[2,512,64]{2,1,0:T(8,128)S(1)}, f32[2,512,64]{2,1,0:T(8,128)S(1)}, u32[]{:S(2)}, u32[]{:S(2)}) %collective-permute-start.6) | collective-permute-done | bytes 262176 | tf_op jit(solution)/shard_map/ppermute | solution.py:27
  98.0 4.8 %collective-permute-start.8 = (f32[2,64,256]{2,1,0:T(8,128)}, f32[2,64,256]{2,1,0:T(8,128)S(1)}, u32[]{:S(2)}, u32[]{:S(2)}) collective-permute-start(f32[2,64,256]{2,1,0:T(8,128)} %get-tuple-element.26), channel_id=1, source_target_pairs={{0,8},{8,16},{16,24},{1,9},{9,17},{17,25},{2,10},{10,18},{18,26},{... | collective-permute-start | bytes 393224 | tf_op jit(solution)/shard_map/ppermute | solution.py:27
  102.8 1.3 collective-permute-start.9
  104.2 2.1 collective-permute-done.9
  107.4 4.8 %collective-permute-start.10 = (f32[2,384,64]{2,1,0:T(8,128)}, f32[2,384,64]{2,1,0:T(8,128)}, u32[]{:S(2)}, u32[]{:S(2)}) collective-permute-start(f32[2,384,64]{2,1,0:T(8,128)} %get-tuple-element.18), channel_id=1, source_target_pairs={{0,1},{1,2},{2,3},{3,4},{4,5},{5,6},{6,7},{8,9},{9,10},{10,11},{11... | collective-permute-start | bytes 589832 | tf_op jit(solution)/shard_map/ppermute | solution.py:27
  112.2 1.5 collective-permute-start.11
  113.7 123.6 %all-reduce.7.cloned.1.call-done = f32[4,2,128,128]{3,2,1,0:T(8,128)} async-done(((f32[4,2,128,128]{3,2,1,0:T(8,128)}), f32[4,2,128,128]{3,2,1,0:T(8,128)}) %all-reduce.7.cloned.1.call-update) | async-done | bytes 524304 | tf_op jit(solution)/shard_map/psum | solution.py:242
  238.4 1.6 pad_maximum_fusion.3.ext
  240.0 24.3 %shard_map.168 = (f32[2,384,384]{2,1,0:T(8,128)S(1)}, f32[4,2,128,128]{3,2,1,0:T(8,128)}) custom-call(s32[16,2]{1,0:T(8,128)S(1)} %copy.18.pos, s32[1]{0:T(128)S(6)} %copy.28.count, f32[2,384,384]{2,1,0:T(8,128)S(1)} %pad_maximum_fusion.3.ext, f32[4,2,128,128]{3,2,1,0:T(8,128)S(1)} %multiply_subtract_fusion.1.probe, f32[16,128,128]{2,1,0:T(8,128)S(1)} %copy-done, ...), custom_call_target="tpu_custom_call" | custom-call | flops 12884901888 | bytes 4456448 | tf_op jit(solution)/shard_map/pallas_call | solution.py:184
  264.4 1.3 collective-permute-start.12
  267.2 3.6 collective-permute-done.13
  271.9 3.5 collective-permute-start.14
  276.8 117.4 %all-reduce.9.cloned.1.call-done = f32[4,2,128,128]{3,2,1,0:T(8,128)} async-done(((f32[4,2,128,128]{3,2,1,0:T(8,128)}), f32[4,2,128,128]{3,2,1,0:T(8,128)}) %all-reduce.9.cloned.1.call-update) | async-done | bytes 524304 | tf_op jit(solution)/shard_map/psum | solution.py:242
  (95 shorter events, 20.1 us)
Async XLA Ops:
  7.2 230.1 %all-reduce.7.cloned.1.call-start = ((), (), s32[]{:S(2)}) async-start(), calls=%async_computation | async-start | bytes 1048576 | tf_op jit(solution)/shard_map/psum | solution.py:242
  8.2 3.8 collective-permute-start
  10.6 5.5 %collective-permute-start.1 = (f32[2,64,256]{2,1,0:T(8,128)S(1)}, f32[2,64,256]{2,1,0:T(8,128)S(1)}, u32[]{:S(2)}, u32[]{:S(2)}) collective-permute-start(f32[2,64,256]{2,1,0:T(8,128)S(1)} %get-tuple-element.28), channel_id=1, source_target_pairs={{8,0},{16,8},{24,16},{9,1},{17,9},{25,17},{10,2},{18,10},{26,18},{... | collective-permute-start | bytes 393224 | tf_op jit(solution)/shard_map/ppermute | solution.py:29
  17.1 19.0 %collective-permute-start.2 = (f32[2,384,64]{2,1,0:T(8,128)}, f32[2,384,64]{2,1,0:T(8,128)}, u32[]{:S(2)}, u32[]{:S(2)}) collective-permute-start(f32[2,384,64]{2,1,0:T(8,128)} %get-tuple-element.20), channel_id=1, source_target_pairs={{0,1},{1,2},{2,3},{3,4},{4,5},{5,6},{6,7},{8,9},{9,10},{10,11},{11... | collective-permute-start | bytes 589832 | tf_op jit(solution)/shard_map/ppermute | solution.py:27
  21.3 14.8 %collective-permute-start.3 = (f32[2,384,64]{2,1,0:T(8,128)S(1)}, f32[2,384,64]{2,1,0:T(8,128)}, u32[]{:S(2)}, u32[]{:S(2)}) collective-permute-start(f32[2,384,64]{2,1,0:T(8,128)S(1)} %get-tuple-element.21), channel_id=1, source_target_pairs={{1,0},{2,1},{3,2},{4,3},{5,4},{6,5},{7,6},{9,8},{10,9},{11,10},{12... | collective-permute-start | bytes 589832 | tf_op jit(solution)/shard_map/ppermute | solution.py:29
  22.7 214.5 %copy-start.8 = (f32[4,1,128,128]{3,2,1,0:T(8,128)}, f32[4,1,128,128]{3,2,1,0:T(8,128)S(1)}, u32[]{:S(2)}) copy-start(f32[4,1,128,128]{3,2,1,0:T(8,128)S(1)} %get-tuple-element.24) | copy-start | bytes 786436
  22.7 214.5 %copy-start.10 = (f32[4,1,128,128]{3,2,1,0:T(8,128)}, f32[4,1,128,128]{3,2,1,0:T(8,128)S(1)}, u32[]{:S(2)}) copy-start(f32[4,1,128,128]{3,2,1,0:T(8,128)S(1)} %get-tuple-element.25) | copy-start | bytes 786436
  62.1 6.0 %collective-permute-start.4 = (f32[2,64,384]{2,1,0:T(8,128)S(1)}, f32[2,64,384]{2,1,0:T(8,128)S(1)}, u32[]{:S(2)}, u32[]{:S(2)}) collective-permute-start(f32[2,64,384]{2,1,0:T(8,128)S(1)} %get-tuple-element.17), channel_id=1, source_target_pairs={{0,8},{8,16},{16,24},{1,9},{9,17},{17,25},{2,10},{10,18},{18,26},{... | collective-permute-start | bytes 589832 | tf_op jit(solution)/shard_map/ppermute | solution.py:27
  66.8 3.3 collective-permute-start.5
  70.4 24.8 %collective-permute-start.6 = (f32[2,512,64]{2,1,0:T(8,128)S(1)}, f32[2,512,64]{2,1,0:T(8,128)S(1)}, u32[]{:S(2)}, u32[]{:S(2)}) collective-permute-start(f32[2,512,64]{2,1,0:T(8,128)S(1)} %get-tuple-element.12), channel_id=1, source_target_pairs={{0,1},{1,2},{2,3},{3,4},{4,5},{5,6},{6,7},{8,9},{9,10},{10,11},{11... | collective-permute-start | bytes 786440 | tf_op jit(solution)/shard_map/ppermute | solution.py:27
  74.5 20.7 %collective-permute-start.7 = (f32[2,512,64]{2,1,0:T(8,128)S(1)}, f32[2,512,64]{2,1,0:T(8,128)S(1)}, u32[]{:S(2)}, u32[]{:S(2)}) collective-permute-start(f32[2,512,64]{2,1,0:T(8,128)S(1)} %get-tuple-element.13), channel_id=1, source_target_pairs={{1,0},{2,1},{3,2},{4,3},{5,4},{6,5},{7,6},{9,8},{10,9},{11,10},{12... | collective-permute-start | bytes 786440 | tf_op jit(solution)/shard_map/ppermute | solution.py:29
  97.2 141.2 %copy-start.6 = (f32[2,256,256]{2,1,0:T(8,128)}, f32[2,256,256]{2,1,0:T(8,128)S(1)}, u32[]{:S(2)}) copy-start(f32[2,256,256]{2,1,0:T(8,128)S(1)} %fusion.11) | copy-start | bytes 1572868
  98.0 6.2 %collective-permute-start.8 = (f32[2,64,256]{2,1,0:T(8,128)}, f32[2,64,256]{2,1,0:T(8,128)S(1)}, u32[]{:S(2)}, u32[]{:S(2)}) collective-permute-start(f32[2,64,256]{2,1,0:T(8,128)} %get-tuple-element.26), channel_id=1, source_target_pairs={{0,8},{8,16},{16,24},{1,9},{9,17},{17,25},{2,10},{10,18},{18,26},{... | collective-permute-start | bytes 393224 | tf_op jit(solution)/shard_map/ppermute | solution.py:27
  102.8 3.5 collective-permute-start.9
  104.1 290.1 %all-reduce.9.cloned.1.call-start = ((), (), s32[]{:S(2)}) async-start(), calls=%async_computation.1 | async-start | bytes 1048576 | tf_op jit(solution)/shard_map/psum | solution.py:242
  107.4 131.0 %collective-permute-start.10 = (f32[2,384,64]{2,1,0:T(8,128)}, f32[2,384,64]{2,1,0:T(8,128)}, u32[]{:S(2)}, u32[]{:S(2)}) collective-permute-start(f32[2,384,64]{2,1,0:T(8,128)} %get-tuple-element.18), channel_id=1, source_target_pairs={{0,1},{1,2},{2,3},{3,4},{4,5},{5,6},{6,7},{8,9},{9,10},{10,11},{11... | collective-permute-start | bytes 589832 | tf_op jit(solution)/shard_map/ppermute | solution.py:27
  112.2 126.2 %collective-permute-start.11 = (f32[2,384,64]{2,1,0:T(8,128)}, f32[2,384,64]{2,1,0:T(8,128)}, u32[]{:S(2)}, u32[]{:S(2)}) collective-permute-start(f32[2,384,64]{2,1,0:T(8,128)} %get-tuple-element.19), channel_id=1, source_target_pairs={{1,0},{2,1},{3,2},{4,3},{5,4},{6,5},{7,6},{9,8},{10,9},{11,10},{12... | collective-permute-start | bytes 589832 | tf_op jit(solution)/shard_map/ppermute | solution.py:29
  264.4 2.6 collective-permute-start.12
  265.8 5.0 %collective-permute-start.13 = (f32[2,64,384]{2,1,0:T(8,128)S(1)}, f32[2,64,384]{2,1,0:T(8,128)S(1)}, u32[]{:S(2)}, u32[]{:S(2)}) collective-permute-start(f32[2,64,384]{2,1,0:T(8,128)S(1)} %get-tuple-element.14), channel_id=1, source_target_pairs={{8,0},{16,8},{24,16},{9,1},{17,9},{25,17},{10,2},{18,10},{26,18},{... | collective-permute-start | bytes 589832 | tf_op jit(solution)/shard_map/ppermute | solution.py:29
  267.2 127.0 %copy-start.9 = (f32[4,1,128,128]{3,2,1,0:T(8,128)S(1)}, f32[4,1,128,128]{3,2,1,0:T(8,128)}, u32[]{:S(2)}) copy-start(f32[4,1,128,128]{3,2,1,0:T(8,128)} %copy-done.8) | copy-start | bytes 786436
  267.2 127.0 %copy-start.11 = (f32[4,1,128,128]{3,2,1,0:T(8,128)S(1)}, f32[4,1,128,128]{3,2,1,0:T(8,128)}, u32[]{:S(2)}) copy-start(f32[4,1,128,128]{3,2,1,0:T(8,128)} %copy-done.10) | copy-start | bytes 786436
  271.9 123.6 %copy-start.18 = (f32[128,128]{1,0:T(8,128)S(1)}, f32[128,128]{1,0:T(8,128)}, u32[]{:S(2)}) copy-start(f32[128,128]{1,0:T(8,128)} %constant.32.clone) | copy-start | bytes 196612
  271.9 124.5 %collective-permute-start.14 = (f32[2,512,64]{2,1,0:T(8,128)}, f32[2,512,64]{2,1,0:T(8,128)S(1)}, u32[]{:S(2)}, u32[]{:S(2)}) collective-permute-start(f32[2,512,64]{2,1,0:T(8,128)} %get-tuple-element.10), channel_id=1, source_target_pairs={{0,1},{1,2},{2,3},{3,4},{4,5},{5,6},{6,7},{8,9},{9,10},{10,11},{11... | collective-permute-start | bytes 786440 | tf_op jit(solution)/shard_map/ppermute | solution.py:27
  275.5 121.0 %collective-permute-start.15 = (f32[2,512,64]{2,1,0:T(8,128)}, f32[2,512,64]{2,1,0:T(8,128)S(1)}, u32[]{:S(2)}, u32[]{:S(2)}) collective-permute-start(f32[2,512,64]{2,1,0:T(8,128)} %get-tuple-element.11), channel_id=1, source_target_pairs={{1,0},{2,1},{3,2},{4,3},{5,4},{6,5},{7,6},{9,8},{10,9},{11,10},{12... | collective-permute-start | bytes 786440 | tf_op jit(solution)/shard_map/ppermute | solution.py:29
  (16 other events, 284.7 us)
Sparse Core Ops, SparseCore 0:
  104.2 132.9 all-reduce.6
  265.9 128.2 all-reduce.8

commit v2 on v1

--- a/solution.py
+++ b/solution.py
@@ -14,23 +14,6 @@
 probe_rate = 2.0
 f32 = jnp.float32
 bf16 = jnp.bfloat16
-
-
-def extended_2(cells, sides, width):
-    for axis, dim in sides:
-        count = lax.axis_size(axis)
-        ends = count - 1
-        head = lax.slice_in_dim(cells, 0, width, axis=dim)
-        tail = lax.slice_in_dim(cells, cells.shape[dim] - width, cells.shape[dim], axis=dim)
-        cells = jnp.concatenate(
-            [
-                lax.ppermute(tail, axis, [(i, (i + 1) % count) for i in range(ends)]),
-                cells,
-                lax.ppermute(head, axis, [((i + 1) % count, i) for i in range(ends)]),
-            ],
-            axis=dim,
-        )
-    return cells
 
 
 def chirp(width):
@@ -175,12 +158,13 @@
     lax.fori_loop(0, slots // step, body, 0)
 
 
-def frame_pass(extended, probe, positions, intensity, count, step=4):
+def frame_pass(extended, probe, positions, intensity, count, step=8):
     modes, _, width, _ = probe.shape
     weights = [jnp.asarray(w) for w in transforms(width)]
     vmem = pl.BlockSpec(memory_space=pltpu.VMEM)
     smem = pl.BlockSpec(memory_space=pltpu.SMEM)
     slots = intensity.shape[0]
+    step = math.gcd(step, slots)
     return pl.pallas_call(
         partial(frames_kernel, modes, width, step),
         out_shape=(
@@ -198,25 +182,312 @@
     )(positions, count, extended, probe, intensity, *weights)
 
 
-def fold_rims(padded, dim, start, length, width):
-    total = padded.shape[dim]
-    core = lax.slice_in_dim(padded, start, start + length, axis=dim)
-    low = lax.slice_in_dim(padded, 0, width, axis=dim)
-    high = lax.slice_in_dim(padded, total - width, total, axis=dim)
-    low_pad = [(0, 0)] * padded.ndim
-    high_pad = [(0, 0)] * padded.ndim
-    low_pad[dim] = (0, length - width)
-    high_pad[dim] = (length - width, 0)
-    return core + jnp.pad(low, low_pad) + jnp.pad(high, high_pad)
-
-
-SIDES = (("rows", 1), ("cols", 2))
-
-
-def return_gradient(gext, tile, width, half):
-    padded = extended_2(gext, SIDES, half)
-    folded = fold_rims(padded, 1, width, tile, half)
-    return fold_rims(folded, 2, width, tile, half)
+MESH = pl.DeviceIdType.MESH
+
+
+def packed(rim):
+    rows = rim.shape[1] // 2
+    return jnp.concatenate([rim[:, :rows], rim[:, rows:]], axis=2)
+
+
+def unpacked(block):
+    half = block.shape[2] // 2
+    return jnp.concatenate([block[:, :, :half], block[:, :, half:]], axis=1)
+
+
+def exchange_kernel(sizes, reduce, give, fetch, names, *refs):
+    n_rows, n_cols, n_z, tile, half, rate = sizes
+    ref = dict(zip(names, refs))
+    row, col = lax.axis_index("rows"), lax.axis_index("cols")
+    core, chip_x = lax.rem(row, 2), row // 2
+    n_y = n_cols // n_z
+    chip_y, chip_z = lax.rem(col, n_y), col // n_y
+    n_b = (n_rows // 2) * n_y
+    place_b = chip_x * n_y + chip_y
+
+    def peers_core():
+        return [(1, 1 - core, (chip_x * 2 + 1 - core, col))]
+
+    def peers_b():
+        out = []
+        for k in range(1, n_b):
+            b = lax.rem(place_b + k, n_b)
+            out.append((k, b, ((b // n_y) * 2 + core, chip_z * n_y + lax.rem(b, n_y))))
+        return out
+
+    def peers_z():
+        out = []
+        for k in range(1, n_z):
+            z = lax.rem(chip_z + k, n_z)
+            out.append((k, z, (row, z * n_y + chip_y)))
+        return out
+
+    sides = {
+        "rows": ((row > 0, (row - 1, col)), (row < n_rows - 1, (row + 1, col))),
+        "cols": ((col > 0, (row, col - 1)), (col < n_cols - 1, (row, col + 1))),
+    }
+
+    barrier = pltpu.get_barrier_semaphore()
+    fixed = peers_core() + peers_b() + peers_z() if reduce else []
+    for _, _, device in fixed:
+        pl.semaphore_signal(barrier, inc=1, device_id=device, device_id_type=MESH)
+    for pair in sides.values():
+        for there, device in pair:
+
+            @pl.when(there)
+            def _():
+                pl.semaphore_signal(barrier, inc=1, device_id=device, device_id_type=MESH)
+
+    beside = sum(there.astype(jnp.int32) for pair in sides.values() for there, _ in pair)
+    pl.semaphore_wait(barrier, beside + len(fixed))
+
+    def sum_probe():
+        grad, full, acc = ref["gprobe"], ref["full"], ref["acc"]
+        size_core = grad.shape[0] // 2
+        size_b = size_core // n_b
+        size_z = size_b // n_z
+        send, recv = ref["r_send"], ref["r_recv"]
+        counter = [0]
+
+        def at(start, size):
+            return pl.ds(pl.multiple_of(start, 8), size)
+
+        def begin(peers, src_of, dst_of):
+            copies = []
+            for k, which, device in peers:
+                copy = pltpu.make_async_remote_copy(
+                    src_ref=src_of(which),
+                    dst_ref=dst_of(k),
+                    send_sem=send.at[counter[0]],
+                    recv_sem=recv.at[counter[0]],
+                    device_id=device,
+                    device_id_type=MESH,
+                )
+                counter[0] += 1
+                copy.start()
+                copies.append(copy)
+            return copies
+
+        base_core = core * size_core
+        base_b = base_core + place_b * size_b
+        base_z = base_b + chip_z * size_z
+        in_core, in_b, in_z = ref["in_core"], ref["in_b"], ref["in_z"]
+        stages = (
+            (peers_core(), grad, 0, size_core, base_core, in_core),
+            (peers_b(), acc, base_core, size_b, base_b, in_b),
+            (peers_z(), acc, base_b, size_z, base_z, in_z),
+        )
+        for peers, source, start, size, mine, landing in stages:
+            copies = begin(
+                peers,
+                lambda which: source.at[at(start + which * size, size)],
+                lambda k: landing.at[k - 1],
+            )
+            yield
+            for copy in copies:
+                copy.wait()
+            value = source[at(mine, size)]
+            for k in range(len(peers)):
+                value = value + landing[k]
+            target = full if landing is in_z else acc
+            target[at(mine, size)] = value
+        for peers, _, _, size, mine, _ in reversed(stages):
+            copies = begin(
+                peers, lambda which: full.at[at(mine, size)], lambda k: full.at[at(mine, size)]
+            )
+            yield
+            for copy in copies:
+                copy.wait()
+        ref["probe_out"][...] = ref["probe"][...] - rate * full[...]
+
+    def swap(side, tag, low, high):
+        (has_low, low_device), (has_high, high_device) = sides[side]
+        from_low, from_high = ref[tag + "_low"], ref[tag + "_high"]
+        sems = ref[tag + "_sems"]
+        to_low = pltpu.make_async_remote_copy(
+            low, from_high, sems.at[0], sems.at[1], device_id=low_device, device_id_type=MESH
+        )
+        to_high = pltpu.make_async_remote_copy(
+            high, from_low, sems.at[2], sems.at[3], device_id=high_device, device_id_type=MESH
+        )
+
+        @pl.when(has_low)
+        def _():
+            to_low.start()
+
+        @pl.when(has_high)
+        def _():
+            to_high.start()
+
+        yield
+
+        @pl.when(has_low)
+        def _():
+            to_low.wait_send()
+            to_high.wait_recv()
+
+        @pl.when(jnp.logical_not(has_low))
+        def _():
+            from_low[...] = jnp.zeros_like(from_low)
+
+        @pl.when(has_high)
+        def _():
+            to_high.wait_send()
+            to_low.wait_recv()
+
+        @pl.when(jnp.logical_not(has_high))
+        def _():
+            from_high[...] = jnp.zeros_like(from_high)
+
+    def together(*parts):
+        for part in parts:
+            next(part)
+        yield
+        for part in parts:
+            next(part, None)
+
+    def move_object():
+        end = tile + half
+        inner = tile - 2 * half
+        if give:
+            gext = ref["gext"]
+            ref["b_to"][0] = packed(gext[:, half:end, :half])
+            ref["b_to"][1] = packed(gext[:, half:end, end:])
+            yield from together(
+                swap("rows", "a", gext.at[:, pl.ds(0, half), :], gext.at[:, pl.ds(end, half), :]),
+                swap("cols", "b", ref["b_to"].at[0], ref["b_to"].at[1]),
+            )
+            a_low, a_high = ref["a_low"][...], ref["a_high"][...]
+            ref["e_to"][0] = jnp.concatenate([a_low[:, :, :half], a_high[:, :, :half]], axis=2)
+            ref["e_to"][1] = jnp.concatenate([a_low[:, :, end:], a_high[:, :, end:]], axis=2)
+            yield from swap("cols", "e", ref["e_to"].at[0], ref["e_to"].at[1])
+            beside = []
+            for name in ("low", "high"):
+                corner = ref["e_" + name][...]
+                beside.append(
+                    unpacked(ref["b_" + name][...])
+                    + jnp.concatenate(
+                        [corner[:, :, :half], jnp.zeros((2, inner, half), f32), corner[:, :, half:]],
+                        axis=1,
+                    )
+                )
+            across = jnp.concatenate(
+                [beside[0], jnp.zeros((2, tile, inner), f32), beside[1]], axis=2
+            )
+            down = jnp.concatenate(
+                [a_low[:, :, half:end], jnp.zeros((2, inner, tile), f32), a_high[:, :, half:end]],
+                axis=1,
+            )
+            grad = gext[:, half:end, half:end] + across + down
+            old = ref["field"][:, half:end, half:end]
+            cells = ref["cells"]
+            cells[...] = old - object_rate * grad
+        else:
+            cells = ref["field"]
+        if fetch:
+            ref["d_to"][0] = packed(cells[:, :, :half])
+            ref["d_to"][1] = packed(cells[:, :, tile - half :])
+            yield from together(
+                swap(
+                    "rows",
+                    "c",
+                    cells.at[:, pl.ds(0, half), :],
+                    cells.at[:, pl.ds(tile - half, half), :],
+                ),
+                swap("cols", "d", ref["d_to"].at[0], ref["d_to"].at[1]),
+            )
+            low, high = unpacked(ref["d_low"][...]), unpacked(ref["d_high"][...])
+            ref["f_to"][0] = jnp.concatenate([low[:, :half], high[:, :half]], axis=2)
+            ref["f_to"][1] = jnp.concatenate([low[:, tile - half :], high[:, tile - half :]], axis=2)
+            yield from swap("rows", "f", ref["f_to"].at[0], ref["f_to"].at[1])
+            ext = ref["ext"]
+            ext[:, half:end, :] = jnp.concatenate([low, cells[...], high], axis=2)
+            for name, start in (("low", 0), ("high", end)):
+                corner = ref["f_" + name][...]
+                ext[:, start : start + half, :] = jnp.concatenate(
+                    [corner[:, :, :half], ref["c_" + name][...], corner[:, :, half:]], axis=2
+                )
+
+    todo = ([sum_probe()] if reduce else []) + [move_object()]
+    while todo:
+        todo = [part for part in todo if next(part, 0) is None]
+
+
+def exchange(ident, tile, half, slots, field, gext=None, gprobe=None, probe=None, fetch=True):
+    reduce = give = gext is not None
+    n_rows, n_cols = lax.axis_size("rows"), lax.axis_size("cols")
+    n_z = 4 if n_cols % 4 == 0 else 1
+    n_b = (n_rows // 2) * (n_cols // n_z)
+    wide = tile + 2 * half
+    vm = lambda *shape: pltpu.VMEM(shape, f32)
+    dma = lambda n: pltpu.SemaphoreType.DMA((n,))
+    names, ops, outs, out_names, scratch = ["field"], [field], [], [], {}
+    shape = None
+    if reduce:
+        shape = probe.shape
+        width = shape[-1]
+        rows = probe.size // width
+        names += ["gext", "gprobe", "probe"]
+        ops += [gext, gprobe.reshape(rows, width), probe.reshape(rows, width)]
+        core = rows // 2
+        count = 2 * (1 + n_b - 1 + n_z - 1)
+        scratch |= {
+            "full": vm(rows, width),
+            "acc": vm(rows, width),
+            "in_core": vm(1, core, width),
+            "in_b": vm(max(n_b - 1, 1), core // n_b, width),
+            "in_z": vm(max(n_z - 1, 1), core // n_b // n_z, width),
+            "r_send": dma(count),
+            "r_recv": dma(count),
+        }
+
+    def lands(tag, *size):
+        return {tag + "_low": vm(*size), tag + "_high": vm(*size), tag + "_sems": dma(4)}
+
+    if give:
+        scratch |= lands("a", 2, half, wide)
+        scratch |= lands("b", 2, tile // 2, 2 * half)
+        scratch |= lands("e", 2, half, 2 * half)
+        scratch["b_to"] = vm(2, 2, tile // 2, 2 * half)
+        scratch["e_to"] = vm(2, 2, half, 2 * half)
+    if fetch:
+        scratch |= lands("c", 2, half, tile)
+        scratch |= lands("d", 2, tile // 2, 2 * half)
+        scratch |= lands("f", 2, half, 2 * half)
+        scratch["d_to"] = vm(2, 2, tile // 2, 2 * half)
+        scratch["f_to"] = vm(2, 2, half, 2 * half)
+        outs.append(jax.ShapeDtypeStruct((2, wide, wide), f32))
+        out_names.append("ext")
+        if give:
+            scratch["cells"] = vm(2, tile, tile)
+    else:
+        outs.append(jax.ShapeDtypeStruct((2, tile, tile), f32))
+        out_names.append("cells")
+    if reduce:
+        outs.append(jax.ShapeDtypeStruct((rows, width), f32))
+        out_names.append("probe_out")
+        rate = probe_rate / (n_rows * n_cols * slots)
+    else:
+        rate = 0.0
+    vmem = pl.BlockSpec(memory_space=pltpu.VMEM)
+    out = pl.pallas_call(
+        partial(
+            exchange_kernel,
+            (n_rows, n_cols, n_z, tile, half, rate),
+            reduce,
+            give,
+            fetch,
+            names + out_names + list(scratch),
+        ),
+        out_shape=tuple(outs),
+        in_specs=[vmem] * len(ops),
+        out_specs=tuple([vmem] * len(outs)),
+        scratch_shapes=list(scratch.values()),
+        compiler_params=pltpu.CompilerParams(
+            collective_id=ident, has_side_effects=True, vmem_limit_bytes=48 * 1024 * 1024
+        ),
+    )(*ops)
+    return out[0], (out[1].reshape(shape) if reduce else None)
 
 
 def times(field, c_real, c_imag):
@@ -229,23 +500,15 @@
     width = probe_modes.shape[-1]
     half = width // 2
     slots = positions.shape[0]
-    row_count = lax.axis_size("rows")
-    col_count = lax.axis_size("cols")
-    frames_all = slots * row_count * col_count
     c_real, c_imag = chirp(width)
     probe = times(probe_modes, c_real, c_imag)
-    tile_field = object_field
-    extended = extended_2(tile_field, SIDES, half)
+    field, _ = exchange(0, tile, half, slots, object_field)
     for it in range(ITERS):
-        last = it == ITERS - 1
-        gext, gprobe = frame_pass(extended, probe, positions, intensity, frame_count)
-        total = lax.psum(gprobe, ("rows", "cols"))
-        probe = probe - probe_rate / frames_all * total
-        gradient = return_gradient(gext, tile, width, half)
-        tile_field = tile_field - object_rate * gradient
-        if not last:
-            extended = extended_2(tile_field, SIDES, half)
-    return (tile_field, times(probe, c_real, -c_imag))
+        gext, gprobe = frame_pass(field, probe, positions, intensity, frame_count)
+        field, probe = exchange(
+            it + 1, tile, half, slots, field, gext, gprobe, probe, fetch=it < ITERS - 1
+        )
+    return (field, times(probe, c_real, -c_imag))
 
 
 def solution(mesh):

time: 407 us -> 120 us (0.29)
  waiting for transfers between devices: 283 us -> 0 us
  Pallas kernels: 48.7 us -> 115 us
  starting transfers between devices: 40.5 us -> 0 us
  between operations: 15.4 us -> 1.52 us
  other arithmetic: 9.73 us -> 2.01 us
  local copies, waits for them, and re-layouts: 8.3 us -> 1.6 us
    psum x2 -> x0, waiting for transfers between devices: 241 us -> none  [body(): total = lax.psum(gprobe, ('rows', 'cols'))]
    pallas_call x0 -> x3, Pallas kernels: none -> 70.9 us  [exchange(): pl.pallas_call(partial(exchange_kernel, (n_rows, n_cols, n_z, tile, half,...]
    ppermute x16 -> x0, waiting for transfers between devices: 42.3 us -> none  [the longest x8 31.8 us: extended_2(): lax.ppermute(tail, axis, [(i, (i + 1) % count) for i in range(ends)])]
    ppermute x16 -> x0, starting transfers between devices: 40.4 us -> none  [the longest x8 29.8 us: extended_2(): lax.ppermute(tail, axis, [(i, (i + 1) % count) for i in range(ends)])]
    slice x10 -> x0, local copies, waits for them, and re-layouts: 5.51 us -> none  [the longest x5 4.18 us: extended_2(): lax.slice_in_dim(cells, cells.shape[dim] - width, cells.shape[dim], axis=...]
    concatenate x5 -> x0, other arithmetic: 4.77 us -> none  [extended_2(): jnp.concatenate([lax.ppermute(tail, axis, [(i, (i + 1) % count) for i in...]
    pallas_call x2, Pallas kernels: 48.7 us -> 44.2 us  [frame_pass(): pl.pallas_call(partial(frames_kernel, modes, width, step), out_shape=(jax...]
  transfers between devices with their start and end apart: 18 -> 0, of which waited for: 8 -> 0; matrix products, arithmetic and copies ran while one was open for 2% -> 0% of each run, Pallas kernels for 0% -> 0%
where the time goes in v2:
time: 120 us
  Pallas kernels  115 us (96%)
  other arithmetic  2.01 us (2%)
  local copies, waits for them, and re-layouts  1.6 us (1%)
  between operations  1.52 us (1%)
    pallas_call x3, Pallas kernels, exchange(): pl.pallas_call(partial(exchange_kernel, (n_rows, n_cols, n_z, tile, half,...  70.9 us
    pallas_call x2, Pallas kernels, frame_pass(): pl.pallas_call(partial(frames_kernel, modes, width, step), out_shape=(jax...  44.2 us

profile of v2, /device:TPU:0, one launch (start us, length us, event | category | flops | bytes accessed | tf_op | source)
XLA Modules:
  0.0 120.2 jit_solution(13499306768093716026)
XLA Ops:
  0.6 0.0 copy-start
  1.3 0.8 copy.18.pos
  2.1 1.1 multiply_subtract_fusion.1
  3.2 0.0 copy-start.1
  3.2 0.0 copy-start.2
  3.2 0.0 copy-start.3
  3.2 0.0 copy-start.4
  3.2 0.0 copy-start.5
  3.3 0.0 copy-done
  3.3 10.7 %shard_map.167.ext.refs_0_ = f32[2,384,384]{2,1,0:T(8,128)S(1)} custom-call(f32[2,256,256]{2,1,0:T(8,128)S(1)} %copy-done), custom_call_target="tpu_custom_call" | custom-call | tf_op jit(solution)/shard_map/pallas_call | solution.py:473
  14.0 0.0 copy-done.1
  14.0 0.0 copy-done.2
  14.1 0.0 copy-done.3
  14.1 0.0 copy-done.4
  14.1 0.0 copy-done.5
  14.1 22.1 %shard_map.168 = (f32[2,384,384]{2,1,0:T(8,128)S(1)}, f32[4,2,128,128]{3,2,1,0:T(8,128)S(1)}) custom-call(s32[16,2]{1,0:T(8,128)S(1)} %copy.18.pos, s32[1]{0:T(128)S(6)} %copy.21.count, f32[2,384,384]{2,1,0:T(8,128)S(1)} %shard_map.167.ext.refs_0_, f32[4,2,128,128]{3,2,1,0:T(8,128)S(1)} %pad_maximum_fusion.probe, f32[16,128,128]{2,1,0:T(8,128)S(1)} %copy-done.1, ...), custom_call_target="tpu_custom_call" | custom-call | flops 12884901888 | bytes 4456448 | tf_op jit(solution)/shard_map/pallas_call | solution.py:168
  36.2 31.7 %shard_map.169 = (f32[2,384,384]{2,1,0:T(8,128)S(1)}, f32[1024,128]{1,0:T(8,128)S(1)}) custom-call(f32[2,384,384]{2,1,0:T(8,128)S(1)} %shard_map.167.ext.refs_0_, f32[2,384,384]{2,1,0:T(8,128)S(1)} %get-tuple-element.10.refs_1_, f32[1024,128]{1,0:T(8,128)S(1)} %bitcast.9, f32[1024,128]{1,0:T(8,128)S(1)} %bitcast.5), custom_call_target="tpu_custom_call" | custom-call | tf_op jit(solution)/shard_map/pallas_call | solution.py:473
  67.9 22.1 %shard_map.170 = (f32[2,384,384]{2,1,0:T(8,128)S(1)}, f32[4,2,128,128]{3,2,1,0:T(8,128)S(1)}) custom-call(s32[16,2]{1,0:T(8,128)S(1)} %copy.18.pos, s32[1]{0:T(128)S(6)} %copy.21.count, f32[2,384,384]{2,1,0:T(8,128)S(1)} %get-tuple-element.12.ext.refs_0_, f32[4,2,128,128]{3,2,1,0:T(8,128)S(1)} %bitcast.7, f32[16,128,128]{2,1,0:T(8,128)S(1)} %copy-done.1, ...), custom_call_target="tpu_custom_call" | custom-call | flops 12884901888 | bytes 4456448 | tf_op jit(solution)/shard_map/pallas_call | solution.py:168
  90.0 0.0 copy-start.6
  90.0 0.0 copy-start.7
  90.0 28.5 %shard_map.171 = (f32[2,256,256]{2,1,0:T(8,128)S(1)}, f32[1024,128]{1,0:T(8,128)S(1)}) custom-call(f32[2,384,384]{2,1,0:T(8,128)S(1)} %get-tuple-element.12.ext.refs_0_, f32[2,384,384]{2,1,0:T(8,128)S(1)} %get-tuple-element.14.refs_1_, f32[1024,128]{1,0:T(8,128)S(1)} %bitcast.8, f32[1024,128]{1,0:T(8,128)S(1)} %get-tuple-element.13.refs_3_), custom_call_target="tpu_custom_call" | custom-call | tf_op jit(solution)/shard_map/pallas_call | solution.py:473
  118.5 0.1 multiply_subtract_fusion
  118.6 0.8 pad_maximum_fusion.1
  119.4 0.8 copy.22
  (3 shorter events, 0.0 us)
Async XLA Ops:
  0.6 2.7 %copy-start = (f32[2,256,256]{2,1,0:T(8,128)S(1)}, f32[2,256,256]{2,1,0:T(8,128)}, u32[]{:S(2)}) copy-start(f32[2,256,256]{2,1,0:T(8,128)} %refs_0_.1) | copy-start | bytes 1572868
  3.2 10.8 %copy-start.1 = (f32[16,128,128]{2,1,0:T(8,128)S(1)}, f32[16,128,128]{2,1,0:T(8,128)}, u32[]{:S(2)}) copy-start(f32[16,128,128]{2,1,0:T(8,128)} %inten.3) | copy-start | bytes 3145732
  3.2 10.8 %copy-start.2 = (bf16[256,768]{1,0:T(8,128)(2,1)S(1)}, bf16[256,768]{1,0:T(8,128)(2,1)}, u32[]{:S(2)}) copy-start(bf16[256,768]{1,0:T(8,128)(2,1)} %constant.19.clone.la) | copy-start | bytes 1179652
  3.2 10.8 %copy-start.3 = (bf16[256,768]{1,0:T(8,128)(2,1)S(1)}, bf16[256,768]{1,0:T(8,128)(2,1)}, u32[]{:S(2)}) copy-start(bf16[256,768]{1,0:T(8,128)(2,1)} %constant.18.clone.lf) | copy-start | bytes 1179652
  3.2 10.8 %copy-start.4 = (bf16[768,256]{1,0:T(8,128)(2,1)S(1)}, bf16[768,256]{1,0:T(8,128)(2,1)}, u32[]{:S(2)}) copy-start(bf16[768,256]{1,0:T(8,128)(2,1)} %constant.17.clone.ra) | copy-start | bytes 1179652
  3.2 10.8 %copy-start.5 = (bf16[768,256]{1,0:T(8,128)(2,1)S(1)}, bf16[768,256]{1,0:T(8,128)(2,1)}, u32[]{:S(2)}) copy-start(bf16[768,256]{1,0:T(8,128)(2,1)} %constant.16.clone.rf) | copy-start | bytes 1179652
  90.0 28.5 %copy-start.6 = (f32[128,128]{1,0:T(8,128)S(1)}, f32[128,128]{1,0:T(8,128)}, u32[]{:S(2)}) copy-start(f32[128,128]{1,0:T(8,128)} %constant.14.clone) | copy-start | bytes 196612
  90.0 28.5 %copy-start.7 = (f32[128,128]{1,0:T(8,128)S(1)}, f32[128,128]{1,0:T(8,128)}, u32[]{:S(2)}) copy-start(f32[128,128]{1,0:T(8,128)} %constant.20.clone) | copy-start | bytes 196612
